TPU v7x, 512 devices: a whole 4x4x16 slice. The times are simulated.
512 devices in a mesh: grain: 64 (over x, z), plane: 8 (over y, core).
Axes of the slice: x: 4, y: 4, z: 16, core: 2. Of those that a mesh axis runs over, the one named last changes fastest.
Arguments:
- field: float32 [262144], P(('plane', 'grain')), may hold values from -16 to 16
- grain_positions: int32 [3, 16384], P(None, 'grain'), may hold values from -79 to 4095, as said below
- pixel_coords: int32 [3, 262144], P(None, 'plane'), may hold values from 0 to 4095, as said below
- block_grain: int32 [8, 2304], P('plane', 'grain'), may hold values from 0 to 3, as said below
- block_pixel: int32 [8, 2304], P('plane', 'grain'), may hold values from 0 to 127, as said below
- block_count: int32 [8, 64], P('plane', 'grain'), may hold values from 4 to 36, as said below
Outputs:
- moments: float32 [3, 16384], P(None, 'grain')
- residual: float32 [262144], P(('plane', 'grain'))
Inputs may be any that keep to these rules, and one draw needn't show every extreme that they name: On each device, the first block_count slots name pairwise distinct pairs (block_grain, block_pixel); later slots hold valid indices and are ignored. `block_pixel`: paired with block_grain slot by slot. `block_count`: some device lists exactly 36 blocks. `grain_positions`: every grain's z is at most 0. `pixel_coords`: every pixel's z is at least 96.
All inputs are finite; a program needn't handle non-finite values.
Results may differ from a plain program's by a relative error of at most 0.0003.
Values sent between devices are 32-bit elements; how exact they have to be, the bound alone decides.
A program may use at most 64 MiB of HBM per device.

v0:
```python
import jax
import jax.numpy as jnp
from jax import lax
from jax.sharding import PartitionSpec as P

BLOCK_G = 64
BLOCK_P = 256
ITERS = 3


field_scale = 27.0
grid_step = 0.03125
blocks_turn = 4


def sensitivities(grain_xyz, pixel_xyz):
    diff = pixel_xyz[:, :, None, :] - grain_xyz[:, :, :, None]
    dist_sq = jnp.sum(diff * diff, axis=0)
    inverse = field_scale / (dist_sq * jnp.sqrt(dist_sq))
    along = 3.0 * diff[2] / dist_sq
    return jnp.stack(
        [along * diff[0] * inverse, along * diff[1] * inverse, (along * diff[2] - 1.0) * inverse]
    )


def local(field, grain_positions, pixel_coords, block_grain, block_pixel, block_count):
    highest = lax.Precision.HIGHEST
    grain_xyz = (grain_positions.astype(jnp.float32) * grid_step).reshape(3, -1, BLOCK_G)
    pixel_xyz = (pixel_coords.astype(jnp.float32) * grid_step).reshape(3, -1, BLOCK_P)
    grain_blocks = grain_xyz.shape[1]
    pixel_blocks = pixel_xyz.shape[1]
    padding = jnp.zeros((blocks_turn,), jnp.int32)
    grain_list = jnp.concatenate([block_grain[0], padding])
    pixel_list = jnp.concatenate([block_pixel[0], padding])
    count = block_count[0, 0]
    turns = (count + blocks_turn - 1) // blocks_turn

    def kernel_turn(turn):
        start = turn * blocks_turn
        gidx = lax.dynamic_slice_in_dim(grain_list, start, blocks_turn)
        pidx = lax.dynamic_slice_in_dim(pixel_list, start, blocks_turn)
        live = (start + jnp.arange(blocks_turn, dtype=jnp.int32) < count).astype(jnp.float32)
        kern = sensitivities(grain_xyz[:, gidx], pixel_xyz[:, pidx])
        return (gidx, pidx, live, kern)

    def forward_part(moment_blocks):

        def forward_step(turn, acc):
            gidx, pidx, live, kern = kernel_turn(turn)
            contrib = (
                jnp.einsum("cbgp,cbg->bp", kern, moment_blocks[:, gidx], precision=highest)
                * live[:, None]
            )
            return acc.at[pidx].add(contrib)

        acc = lax.fori_loop(0, turns, forward_step, jnp.zeros((pixel_blocks, BLOCK_P), jnp.float32))
        return acc.reshape(-1)

    def backward_part(values):
        rows = values.reshape(pixel_blocks, BLOCK_P)

        def backward_step(turn, acc):
            gidx, pidx, live, kern = kernel_turn(turn)
            contrib = jnp.einsum(
                "cbgp,bp->cbg", kern, rows[pidx] * live[:, None], precision=highest
            )
            return acc.at[:, gidx].add(contrib)

        acc = lax.fori_loop(
            0, turns, backward_step, jnp.zeros((3, grain_blocks, BLOCK_G), jnp.float32)
        )
        return lax.psum(acc, "plane")

    def apply_backward(values):
        return backward_part(lax.all_gather(values, "grain", axis=0, tiled=True))

    residual = field
    moments = jnp.zeros((3, grain_blocks, BLOCK_G), jnp.float32)

    def squared_norm(grad):
        return lax.psum(jnp.sum(grad * grad), "grain")

    grad = apply_backward(residual)
    direction = grad
    gamma = squared_norm(grad)
    for step_index in range(ITERS):
        image = lax.psum_scatter(forward_part(direction), "grain", scatter_dimension=0, tiled=True)
        delta = lax.psum(jnp.sum(image * image), ("grain", "plane"))
        alpha = gamma / delta
        moments = moments + alpha * direction
        residual = residual - alpha * image
        if step_index + 1 < ITERS:
            grad = apply_backward(residual)
            gamma_next = squared_norm(grad)
            direction = grad + gamma_next / gamma * direction
            gamma = gamma_next
    return (moments.reshape(3, -1), residual)


def solution(mesh):
    placed = (
        P(("plane", "grain")),
        P(None, "grain"),
        P(None, "plane"),
        P("plane", "grain"),
        P("plane", "grain"),
        P("plane", "grain"),
    )
    return jax.shard_map(
        local,
        mesh=mesh,
        in_specs=placed,
        out_specs=(P(None, "grain"), P(("plane", "grain"))),
        check_vma=False,
    )
```

profile of v0, /device:TPU:1, one launch (start us, length us, event | category | flops | bytes accessed | tf_op | source)
XLA Modules:
  0.0 1903.3 jit_solution(15638585753216149469)
XLA Ops:
  7.9 1.2 convert_multiply_fusion
  10.5 0.7 copy-done
  11.2 80.8 %all-gather = f32[64,1,512]{2,1,0:T(1,128)S(1)} all-gather(f32[1,1,512]{2,1,0:T(1,128)S(1)} %bitcast.237), channel_id=1, replica_groups=mesh['grain'=64,'plane'=8] {'grain'}, dimensions={0}, use_global_device_ids=true | all-gather | bytes 133120 | tf_op jit(solution)/shard_map/all_gather | solution.py:75
  92.3 13.7 while.72
  95.3 1.0 fusion.87
  96.2 0.7 scatter_fusion
  99.9 1.0 fusion.87
  104.4 1.0 fusion.87
  105.4 0.7 scatter_fusion
  106.1 57.2 %psum.63 = f32[3,4,64]{2,0,1:T(4,128)S(1)} all-reduce(f32[3,4,64]{2,0,1:T(4,128)S(1)} %get-tuple-element.698), channel_id=1, replica_groups=mesh['grain'=64,'plane'=8] {'plane'}, use_global_device_ids=true, to_apply=%region_4.5 | all-reduce | flops 768 | bytes 6144 | tf_op jit(solution)/shard_map/psum | solution.py:72
  163.3 12.6 while.73
  166.0 0.7 compare_convert_fusion.13
  166.7 0.8 scatter_custom_fusion.20
  170.2 0.7 compare_convert_fusion.13
  170.9 0.8 scatter_custom_fusion.20
  174.4 0.7 compare_convert_fusion.13
  175.1 0.8 scatter_custom_fusion.20
  175.8 0.7 copy.96
  177.2 133.5 %psum.64 = f32[]{:T(128)} all-reduce(f32[]{:T(128)} %multiply_reduce_fusion.8), channel_id=1, replica_groups=mesh['grain'=64,'plane'=8] {'grain'}, use_global_device_ids=true, to_apply=%region_6.7 | all-reduce | flops 1 | bytes 8 | tf_op jit(solution)/shard_map/psum | solution.py:81
  310.7 1.3 dynamic-slice
  312.6 139.8 %all-reduce.9.cloned.1.call-done = f32[32768]{0:T(1024)} async-done(((f32[32768]{0:T(1024)}), f32[32768]{0:T(1024)}) %all-reduce.9.cloned.1.call-update) | async-done | bytes 131088
  452.5 1.4 multiply_reduce_fusion.11
  453.8 110.3 %psum.65 = f32[]{:T(128)} all-reduce(f32[]{:T(128)} %multiply_reduce_fusion.11), channel_id=1, replica_groups=mesh['grain'=64,'plane'=8] {'grain','plane'}, use_global_device_ids=true, to_apply=%region_13.14 | all-reduce | flops 1 | bytes 8 | tf_op jit(solution)/shard_map/psum | solution.py:88
  565.4 0.8 multiply_subtract_fusion.2
  566.1 71.8 %all-gather.1 = f32[64,1,512]{2,1,0:T(1,128)S(1)} all-gather(f32[1,1,512]{2,1,0:T(1,128)S(1)} %bitcast.236), channel_id=1, replica_groups=mesh['grain'=64,'plane'=8] {'grain'}, dimensions={0}, use_global_device_ids=true | all-gather | bytes 133120 | tf_op jit(solution)/shard_map/all_gather | solution.py:75
  638.3 13.7 while.74
  641.3 1.0 fusion.95
  642.2 0.7 scatter_fusion.1
  645.8 1.0 fusion.95
  650.4 1.0 fusion.95
  651.4 0.7 scatter_fusion.1
  652.1 54.9 %psum.66 = f32[3,4,64]{2,0,1:T(4,128)S(1)} all-reduce(f32[3,4,64]{2,0,1:T(4,128)S(1)} %get-tuple-element.700), channel_id=1, replica_groups=mesh['grain'=64,'plane'=8] {'plane'}, use_global_device_ids=true, to_apply=%region_18.19 | all-reduce | flops 768 | bytes 6144 | tf_op jit(solution)/shard_map/psum | solution.py:72
  707.5 111.8 %psum.67 = f32[]{:T(128)} all-reduce(f32[]{:T(128)} %multiply_reduce_fusion.7), channel_id=1, replica_groups=mesh['grain'=64,'plane'=8] {'grain'}, use_global_device_ids=true, to_apply=%region_20.21 | all-reduce | flops 1 | bytes 8 | tf_op jit(solution)/shard_map/psum | solution.py:81
  820.7 12.6 while.75
  823.5 0.7 compare_convert_fusion.15
  824.1 0.8 scatter_custom_fusion.23
  828.3 0.8 scatter_custom_fusion.23
  832.5 0.8 scatter_custom_fusion.23
  833.3 0.7 copy.97
  834.1 283.0 %all-reduce.11.cloned.1.call-done = f32[32768]{0:T(1024)} async-done(((f32[32768]{0:T(1024)}), f32[32768]{0:T(1024)}) %all-reduce.11.cloned.1.call-update) | async-done | bytes 131088
  1117.0 1.4 multiply_reduce_fusion.10
  1118.4 110.3 %psum.68 = f32[]{:T(128)} all-reduce(f32[]{:T(128)} %multiply_reduce_fusion.10), channel_id=1, replica_groups=mesh['grain'=64,'plane'=8] {'grain','plane'}, use_global_device_ids=true, to_apply=%region_27.28 | all-reduce | flops 1 | bytes 8 | tf_op jit(solution)/shard_map/psum | solution.py:88
  1230.0 0.8 multiply_subtract_fusion.1
  1230.7 71.8 %all-gather.2 = f32[64,1,512]{2,1,0:T(1,128)S(1)} all-gather(f32[1,1,512]{2,1,0:T(1,128)S(1)} %bitcast.235), channel_id=1, replica_groups=mesh['grain'=64,'plane'=8] {'grain'}, dimensions={0}, use_global_device_ids=true | all-gather | bytes 133120 | tf_op jit(solution)/shard_map/all_gather | solution.py:75
  1302.9 13.7 while.76
  1305.8 1.0 fusion.103
  1306.8 0.7 scatter_fusion.2
  1310.4 1.0 fusion.103
  1315.0 1.0 fusion.103
  1316.0 0.7 scatter_fusion.2
  1316.6 54.9 %psum.69 = f32[3,4,64]{2,0,1:T(4,128)S(1)} all-reduce(f32[3,4,64]{2,0,1:T(4,128)S(1)} %get-tuple-element.702), channel_id=1, replica_groups=mesh['grain'=64,'plane'=8] {'plane'}, use_global_device_ids=true, to_apply=%region_32.33 | all-reduce | flops 768 | bytes 6144 | tf_op jit(solution)/shard_map/psum | solution.py:72
  1371.5 0.7 multiply_reduce_fusion.6
  1372.2 111.9 %psum.70 = f32[]{:T(128)} all-reduce(f32[]{:T(128)} %multiply_reduce_fusion.6), channel_id=1, replica_groups=mesh['grain'=64,'plane'=8] {'grain'}, use_global_device_ids=true, to_apply=%region_34.35 | all-reduce | flops 1 | bytes 8 | tf_op jit(solution)/shard_map/psum | solution.py:81
  1485.4 12.6 while.77
  1488.1 0.7 compare_convert_fusion.17
  1488.8 0.8 scatter_custom_fusion.26
  1493.0 0.8 scatter_custom_fusion.26
  1497.2 0.8 scatter_custom_fusion.26
  1497.9 0.7 copy.98
  1498.7 283.0 %all-reduce.13.cloned.1.call-done = f32[32768]{0:T(1024)} async-done(((f32[32768]{0:T(1024)}), f32[32768]{0:T(1024)}) %all-reduce.13.cloned.1.call-update) | async-done | bytes 131088
  1781.7 1.4 multiply_reduce_fusion.9
  1783.1 110.3 %psum.71 = f32[]{:T(128)} all-reduce(f32[]{:T(128)} %multiply_reduce_fusion.9), channel_id=1, replica_groups=mesh['grain'=64,'plane'=8] {'grain','plane'}, use_global_device_ids=true, to_apply=%region_41.42 | all-reduce | flops 1 | bytes 8 | tf_op jit(solution)/shard_map/psum | solution.py:88
  1894.7 0.7 reshape.219
  1895.4 1.3 multiply_subtract_fusion
  (259 shorter events, 58.8 us)
Async XLA Ops:
  7.2 445.3 %all-reduce.9.cloned.1.call-start = ((), (), s32[]{:S(2)}) async-start(), calls=%async_computation | async-start | bytes 262144
  7.9 1.2 copy-start.1
  9.2 0.7 copy-start.2
  9.8 0.7 copy-start.3
  10.5 0.7 copy-start
  176.6 940.5 %all-reduce.11.cloned.1.call-start = ((), (), s32[]{:S(2)}) async-start(), calls=%async_computation.1 | async-start | bytes 262144
  834.0 947.7 %all-reduce.13.cloned.1.call-start = ((), (), s32[]{:S(2)}) async-start(), calls=%async_computation.2 | async-start | bytes 262144
Sparse Core Ops, SparseCore 0:
  176.7 275.7 all-reduce.8
  834.1 282.8 all-reduce.10
  1498.8 282.8 all-reduce.12
where the time goes:
time: 1900 us
  blocking collectives  1080 us (57%)
  waiting for transfers between devices  706 us (37%)
  other arithmetic  44.2 us (2%)
  local copies, waits for them, and re-layouts  37.4 us (2%)
  between operations  21.7 us (1%)
    unnamed x6, waiting for transfers between devices  706 us
    psum x3, blocking collectives, squared_norm(): return lax.psum(jnp.sum(grad * grad), 'grain')  357 us
    psum x3, blocking collectives, local(): delta = lax.psum(jnp.sum(image * image), ('grain', 'plane'))  331 us
    all_gather x3, blocking collectives, apply_backward(): return backward_part(lax.all_gather(values, 'grain', axis=0, tiled=True))  224 us
    psum x3, blocking collectives, backward_part(): return lax.psum(acc, 'plane')  167 us
  transfers between devices with their start and end apart: 3, of which 3 were waited for; matrix products, arithmetic and copies ran while one was open for 0% of the time, Pallas kernels for 0%

commit v1 on v0

v1 whole, which is shorter than its diff:
```python
import functools

import jax
import jax.numpy as jnp
from jax import lax
from jax.experimental import pallas as pl
from jax.experimental.pallas import tpu as pltpu
from jax.sharding import PartitionSpec as P

MESH = pl.DeviceIdType.MESH
BLOCK_G = 64
ITERS = 3
SLOTS = 36
GROUPS = 8
F32 = jnp.float32


def tables(block_grain, block_pixel, block_count):
    slot = jnp.arange(SLOTS, dtype=jnp.int32)
    live = slot < block_count[0, 0]
    key = jnp.where(live, block_grain[0], 4)
    before = (key[None, :] < key[:, None]) | ((key[None, :] == key[:, None]) & (slot[None, :] < slot[:, None]))
    rank = jnp.sum(before.astype(jnp.int32), axis=1)
    place = (rank[None, :] == slot[:, None]).astype(jnp.int32)
    pixel = jnp.sum(place * block_pixel[0][None, :], axis=1)
    grain = jnp.minimum(jnp.sum(place * key[None, :], axis=1), 3)
    alive = jnp.sum(place * live.astype(jnp.int32)[None, :], axis=1)
    upto = jnp.sum((key[None, :] <= grain[:, None]).astype(jnp.int32), axis=1)
    below = jnp.sum((key[None, :] < grain[:, None]).astype(jnp.int32), axis=1)
    same = ((slot > below) | (alive == 0)).astype(jnp.int32)
    same = jnp.where((slot == 0), 0, same)
    each = jnp.arange(SLOTS, dtype=jnp.int32)
    last = jnp.maximum(jnp.sum((key[None, :] <= each[:, None]).astype(jnp.int32), axis=1) - 1, 0)
    held = (jnp.sum((key[None, :] == each[:, None]).astype(jnp.int32), axis=1) > 0).astype(jnp.int32)
    del upto
    table = jnp.stack([pixel, grain, alive, same, last, held])
    half = jnp.arange(2, dtype=jnp.int32)
    target = jnp.where(alive[:, None] > 0, 2 * pixel[:, None] + half[None, :], -1).reshape(1, 2 * SLOTS)
    target = jnp.concatenate([target, jnp.full((1, 128 - 2 * SLOTS), -1, jnp.int32)], axis=1)
    return table, target


def kernel(
    sizes,
    table,
    target,
    field,
    grains,
    pixels,
    moments_out,
    residual_out,
    coords,
    sens,
    spread,
    snap,
    picks,
    contrib,
    rows,
    gather_send,
    gathered,
    part_send,
    part_recv,
    grad_send,
    grad_recv,
    gamma_send,
    gamma_recv,
    norm_send,
    norm_recv,
    total_send,
    total_recv,
    gather_sem,
    part_sem,
    grad_sem,
    gamma_sem,
    last_sem,
):
    nx, nz, npl = sizes
    ng = nx * nz
    far = nz // 2
    g, p = lax.axis_index("grain"), lax.axis_index("plane")
    x, z = g // nz, lax.rem(g, nz)

    def grain_peer(i):
        m = i // nx
        a = lax.rem(i + 1, nx)
        d = far + (1 - 2 * lax.rem(m, 2)) * ((m + 1) // 2)
        return lax.rem(x + a, nx) * nz + lax.rem(z + d, nz)

    def plane_peer(i):
        return lax.rem(p + i + 1, npl)

    def each(n, body):
        def step(i, carry):
            body(i)
            return carry

        lax.fori_loop(0, n, step, 0)

    def to_grains(source, place, send_sem, recv_sem):
        def send(i):
            peer = grain_peer(i)
            pltpu.make_async_remote_copy(
                src_ref=source(peer),
                dst_ref=place(i),
                send_sem=send_sem,
                recv_sem=recv_sem,
                device_id=(peer, p),
                device_id_type=MESH,
            ).start()

        each(ng - 1, send)

    def to_planes(source, place, send_sem, recv_sem):
        def send(i):
            pltpu.make_async_remote_copy(
                src_ref=source,
                dst_ref=place(i),
                send_sem=send_sem,
                recv_sem=recv_sem,
                device_id=(g, plane_peer(i)),
                device_id_type=MESH,
            ).start()

        each(npl - 1, send)

    def wait(ref, sem):
        pltpu.make_async_copy(ref, ref, sem).wait()

    barrier = pltpu.get_barrier_semaphore()
    each(
        ng - 1,
        lambda i: pl.semaphore_signal(barrier, inc=1, device_id=(grain_peer(i), p), device_id_type=MESH),
    )
    each(
        npl - 1,
        lambda i: pl.semaphore_signal(barrier, inc=1, device_id=(g, plane_peer(i)), device_id_type=MESH),
    )

    lane = lax.broadcasted_iota(jnp.int32, (8, 128), 1)

    def broadcast_lanes(tile):
        for r in range(96):
            c, b, k = r // 32, r // 8 % 4, r % 8
            spread[b, c, k] = jnp.broadcast_to(tile[:, r : r + 1], (8, 128))

    broadcast_lanes(grains[...].astype(F32) * 0.03125)
    picks[...] = (lax.broadcasted_iota(jnp.int32, (4 * ng, 128), 0) == target[...]).astype(F32)
    contrib[...] = jnp.zeros((128, 128), F32)

    for c in range(3):
        coords[c] = (pixels[c : c + 1, :].astype(F32) * 0.03125).reshape(4 * ng, 128)

    def make_sens(j):
        e, b = table[0, j], table[1, j]
        scale = table[2, j].astype(F32) * 27.0
        for h in range(2):
            px, py, pz = (coords[c, pl.ds(2 * e + h, 1), :] for c in range(3))
            for k in range(GROUPS):
                dx = px - spread[b, 0, k]
                dy = py - spread[b, 1, k]
                dz = pz - spread[b, 2, k]
                inv = lax.rsqrt(dx * dx + dy * dy + dz * dz)
                inv2 = inv * inv
                inv3 = inv2 * inv * scale
                along = 3.0 * dz * inv2 * inv3
                sens[j, 0, k, h] = along * dx
                sens[j, 1, k, h] = along * dy
                sens[j, 2, k, h] = along * dz - inv3

    def gather(it):
        to_grains(lambda peer: gather_send.at[it], lambda i: gathered.at[it, g], gather_sem.at[0, it], gather_sem.at[1, it])
        gathered[it, g] = gather_send[it]

    def gather_wait(it):
        wait(gathered.at[it, pl.ds(0, ng - 1)], gather_sem.at[1, it])

    def backward():
        def step(j, acc):
            e = table[0, j]
            keep = table[3, j].astype(F32)
            v0 = jnp.broadcast_to(rows[pl.ds(2 * e, 1), :], (8, 128))
            v1 = jnp.broadcast_to(rows[pl.ds(2 * e + 1, 1), :], (8, 128))
            out = []
            for c in range(3):
                for k in range(GROUPS):
                    i = c * GROUPS + k
                    t = acc[i] * keep + (sens[j, c, k, 0] * v0 + sens[j, c, k, 1] * v1)
                    snap[j, i] = t
                    out.append(t)
            return tuple(out)

        lax.fori_loop(0, SLOTS, step, tuple(jnp.zeros((8, 128), F32) for _ in range(24)))
        total = jnp.zeros((8, 128), F32)
        for b in range(4):
            last = table[4, b]
            held = table[5, b].astype(F32)
            for i in range(24):
                s = jnp.sum(snap[last, i], axis=1, keepdims=True) * held
                total = jnp.where(lane == (i // 8) * 32 + b * 8 + i % 8, s, total)
        return total

    def forward(it):
        def step(j, carry):
            b = table[1, j]
            acc = [[jnp.zeros((8, 128), F32) for _ in range(2)] for _ in range(2)]
            for c in range(3):
                for k in range(GROUPS):
                    d = spread[b, c, k]
                    for h in range(2):
                        acc[h][k % 2] = acc[h][k % 2] + sens[j, c, k, h] * d
            for h in range(2):
                contrib[pl.ds(2 * j + h, 1), :] = jnp.sum(acc[h][0] + acc[h][1], axis=0, keepdims=True)
            return carry

        lax.fori_loop(0, SLOTS, step, 0)
        part = jnp.dot(picks[...], contrib[...], precision=lax.Precision.HIGHEST, preferred_element_type=F32)
        part_send[it] = part.reshape(ng, 4, 128)
        to_grains(lambda peer: part_send.at[it, peer], lambda i: part_recv.at[it, i], part_sem.at[0, it], part_sem.at[1, it])
        wait(part_recv.at[it], part_sem.at[1, it])
        return jnp.sum(part_recv[it], axis=0) + part_send[it, g]

    def plane_sum(it, tile):
        grad_send[it] = tile
        to_planes(grad_send.at[it], lambda i: grad_recv.at[it, i], grad_sem.at[0, it], grad_sem.at[1, it])
        wait(grad_recv.at[it], grad_sem.at[1, it])
        return tile + jnp.sum(grad_recv[it], axis=0)

    def full_sum(tile):
        return jnp.sum(jnp.sum(tile, axis=0, keepdims=True), axis=1, keepdims=True)

    gather_send[0] = field[...]
    pl.semaphore_wait(barrier, ng - 1 + npl - 1)
    gather(0)
    each(SLOTS, make_sens)
    gather_wait(0)
    rows[...] = gathered[0].reshape(4 * ng, 128)

    grad = plane_sum(0, backward())
    residual = field[...]
    moments = direction = jnp.zeros((8, 128), F32)
    image = jnp.zeros((4, 128), F32)
    gamma = jnp.ones((1, 1), F32)
    for it in range(ITERS):
        mine = full_sum(grad * grad)
        gamma_send[it] = jnp.broadcast_to(mine, (1, 128))
        to_grains(lambda peer: gamma_send.at[it], lambda i: gamma_recv.at[it, i], gamma_sem.at[0, it], gamma_sem.at[1, it])
        broadcast_lanes(grad)
        image_new = forward(it)
        wait(gamma_recv.at[it], gamma_sem.at[1, it])
        gamma_new = mine + jnp.sum(gamma_recv[it], axis=0)[:, 0:1]
        if it == 0:
            direction, image = grad, image_new
        else:
            beta = gamma_new / gamma
            direction = grad + beta * direction
            image = image_new + beta * image
        gamma = gamma_new
        if it + 1 < ITERS:
            gather_send[it + 1] = image
            gather(it + 1)
            gather_wait(it + 1)
            full = gathered[it + 1].reshape(4 * ng, 128)
            rows[...] = full
            tile = jnp.where(lane >= 96, full_sum(full * full), backward())
            tile = plane_sum(it + 1, tile)
            alpha = gamma / tile[0:1, 96:97]
            moments = moments + alpha * direction
            residual = residual - alpha * image
            grad = jnp.where(lane >= 96, 0.0, grad - alpha * tile)
        else:
            norm = full_sum(image * image)
            norm_send[...] = jnp.broadcast_to(norm, (1, 128))
            to_planes(norm_send, lambda i: norm_recv.at[i], last_sem.at[0], last_sem.at[1])
            wait(norm_recv, last_sem.at[1])
            over_planes = norm + jnp.sum(norm_recv[...], axis=0)[:, 0:1]
            total_send[...] = jnp.broadcast_to(over_planes, (1, 128))
            to_grains(lambda peer: total_send, lambda i: total_recv.at[i], last_sem.at[2], last_sem.at[3])
            wait(total_recv, last_sem.at[3])
            alpha = gamma / (over_planes + jnp.sum(total_recv[...], axis=0)[:, 0:1])
            moments_out[...] = moments + alpha * direction
            residual_out[...] = residual - alpha * image

    for it in range(ITERS):
        wait(gathered.at[it, pl.ds(0, ng - 1)], gather_sem.at[0, it])
        wait(part_recv.at[it], part_sem.at[0, it])
        wait(grad_recv.at[it], grad_sem.at[0, it])
        wait(gamma_recv.at[it], gamma_sem.at[0, it])
    wait(norm_recv, last_sem.at[0])
    wait(total_recv, last_sem.at[2])


def local(sizes, field, grain_positions, pixel_coords, block_grain, block_pixel, block_count):
    nx, nz, npl = sizes
    ng = nx * nz
    table, target = tables(block_grain, block_pixel, block_count)
    grains = grain_positions.reshape(3, 32, 8).transpose(2, 0, 1).reshape(8, 96)
    grains = jnp.concatenate([grains, jnp.zeros((8, 32), jnp.int32)], axis=1)
    vmem = pl.BlockSpec(memory_space=pltpu.VMEM)
    moments, residual = pl.pallas_call(
        functools.partial(kernel, sizes),
        out_shape=(jax.ShapeDtypeStruct((8, 128), F32), jax.ShapeDtypeStruct((4, 128), F32)),
        in_specs=[pl.BlockSpec(memory_space=pltpu.SMEM)] + [vmem] * 4,
        out_specs=(vmem, vmem),
        scratch_shapes=[
            pltpu.VMEM((3, 4 * ng, 128), F32),
            pltpu.VMEM((SLOTS, 3, GROUPS, 2, 8, 128), F32),
            pltpu.VMEM((4, 3, GROUPS, 8, 128), F32),
            pltpu.VMEM((SLOTS, 24, 8, 128), F32),
            pltpu.VMEM((4 * ng, 128), F32),
            pltpu.VMEM((128, 128), F32),
            pltpu.VMEM((4 * ng, 128), F32),
            pltpu.VMEM((ITERS, 4, 128), F32),
            pltpu.VMEM((ITERS, ng, 4, 128), F32),
            pltpu.VMEM((ITERS, ng, 4, 128), F32),
            pltpu.VMEM((ITERS, ng - 1, 4, 128), F32),
            pltpu.VMEM((ITERS, 8, 128), F32),
            pltpu.VMEM((ITERS, npl - 1, 8, 128), F32),
            pltpu.VMEM((ITERS, 1, 128), F32),
            pltpu.VMEM((ITERS, ng - 1, 1, 128), F32),
            pltpu.VMEM((1, 128), F32),
            pltpu.VMEM((npl - 1, 1, 128), F32),
            pltpu.VMEM((1, 128), F32),
            pltpu.VMEM((ng - 1, 1, 128), F32),
            pltpu.SemaphoreType.DMA((2, ITERS)),
            pltpu.SemaphoreType.DMA((2, ITERS)),
            pltpu.SemaphoreType.DMA((2, ITERS)),
            pltpu.SemaphoreType.DMA((2, ITERS)),
            pltpu.SemaphoreType.DMA((4,)),
        ],
        compiler_params=pltpu.CompilerParams(collective_id=1, has_side_effects=True, vmem_limit_bytes=40 << 20),
        name="solve",
    )(table, target, field.reshape(4, 128), grains, pixel_coords)
    moments = moments[:, :96].reshape(8, 3, 32).transpose(1, 2, 0).reshape(3, 256)
    return moments, residual.reshape(512)


def solution(mesh, rows=4):
    grain, plane = mesh.shape["grain"], mesh.shape["plane"]
    placed = (
        P(("plane", "grain")),
        P(None, "grain"),
        P(None, "plane"),
        P("plane", "grain"),
        P("plane", "grain"),
        P("plane", "grain"),
    )
    return jax.shard_map(
        functools.partial(local, (rows, grain // rows, plane)),
        mesh=mesh,
        in_specs=placed,
        out_specs=(P(None, "grain"), P(("plane", "grain"))),
        check_vma=False,
    )
```

time: 1900 us -> 122 us (0.06)
  blocking collectives: 1080 us -> 0 us
  waiting for transfers between devices: 706 us -> 0 us
  Pallas kernels: 0 us -> 114 us
  other arithmetic: 44.2 us -> 0.64 us
  local copies, waits for them, and re-layouts: 37.4 us -> 5.31 us
  between operations: 21.7 us -> 1.37 us
    psum x9 -> x0, blocking collectives: 855 us -> none  [the longest x3 357 us: squared_norm(): return lax.psum(jnp.sum(grad * grad), 'grain')]
    unnamed x6 -> x0, waiting for transfers between devices: 706 us -> none
    all_gather x3 -> x0, blocking collectives: 224 us -> none  [apply_backward(): return backward_part(lax.all_gather(values, 'grain', axis=0, tiled=True))]
    pallas_call x0 -> x1, Pallas kernels: none -> 114 us  [local(): pl.pallas_call(functools.partial(kernel, sizes), out_shape=(jax.ShapeDtyp...]
    gather x90 -> x0, local copies, waits for them, and re-layouts: 31 us -> none  [the longest x72 20.8 us: kernel_turn(): kern = sensitivities(grain_xyz[:, gidx], pixel_xyz[:, pidx])]
  transfers between devices with their start and end apart: 3 -> 0, of which waited for: 3 -> 0; matrix products, arithmetic and copies ran while one was open for 0% -> 0% of each run, Pallas kernels for 0% -> 0%
where the time goes in v1:
time: 122 us; the launch traced here: 121 us
  Pallas kernels  114 us (93%)
  local copies, waits for them, and re-layouts  5.31 us (4%)
  between operations  1.37 us (1%)
    pallas_call x1, Pallas kernels, local(): pl.pallas_call(functools.partial(kernel, sizes), out_shape=(jax.ShapeDtyp...  114 us
    unnamed x11, local copies, waits for them, and re-layouts  4.17 us

profile of v1, /device:TPU:1, one launch (start us, length us, event | category | flops | bytes accessed | tf_op | source)
XLA Modules:
  0.0 121.3 jit_solution(3389006182001477728)
XLA Ops:
  1.3 0.0 copy-start.4
  1.3 0.6 copy-done.4
  1.9 0.2 convert_reduce_fusion
  2.2 0.0 copy-start.3
  2.2 0.6 copy-done.3
  2.8 0.1 select_reduce_fusion
  3.0 0.2 convert_reduce_fusion.2
  3.2 0.1 add_select_fusion
  3.3 0.0 copy-start.2
  3.3 0.1 select_n.40
  3.4 0.6 copy-done.2
  4.0 0.1 reshape.161
  4.1 0.1 copy.14
  4.1 0.0 copy-start.1
  4.1 0.7 copy-done.1
  4.8 0.0 copy-start
  4.8 1.0 copy-done
  5.9 114.0 %solve.1 = (f32[8,128]{1,0:T(8,128)S(1)}, f32[4,128]{1,0:T(4,128)S(1)}) custom-call(s32[6,36]{1,0:T(8,128)S(1)} %stack.15.table, s32[1,128]{1,0:T(1,128)S(1)} %concatenate.6.target, f32[4,128]{1,0:T(4,128)S(1)} %bitcast.28, s32[8,128]{1,0:T(8,128)S(1)} %concatenate.7.grains, s32[3,32768]{1,0:T(4,128)S(1)} %copy-done), custom_call_target="tpu_custom_call" | custom-call | tf_op jit(solution)/shard_map/solve/pallas_call | solution.py:299
  119.9 0.1 reshape.163
  120.0 0.1 copy.13
  120.1 0.7 reshape.164
  120.8 0.6 copy.17
  (11 shorter events, 0.1 us)
Async XLA Ops:
  1.3 0.7 copy-start.4
  2.2 0.7 copy-start.3
  3.3 0.7 copy-start.2
  4.1 0.7 copy-start.1
  4.8 1.0 copy-start

commit v2 on v1

v2 whole, which is shorter than its diff:
```python
import functools

import jax
import jax.numpy as jnp
from jax import lax
from jax.experimental import pallas as pl
from jax.experimental.pallas import tpu as pltpu
from jax.sharding import PartitionSpec as P

MESH = pl.DeviceIdType.MESH
BLOCK_G = 64
ITERS = 3
SLOTS = 36
GROUPS = 8
F32 = jnp.float32


def kernel(
    sizes,
    field_in,
    grains_in,
    pixels_in,
    block_grain_in,
    block_pixel_in,
    block_count_in,
    moments_out,
    residual_out,
    field,
    grains,
    pixels,
    block_grain,
    block_pixel,
    block_count,
    table_made,
    table,
    coords,
    sens,
    spread,
    snap,
    picks,
    unfold,
    contrib,
    rows,
    gather_send,
    gathered,
    part_send,
    part_recv,
    grad_send,
    grad_recv,
    norm_send,
    norm_recv,
    total_send,
    total_recv,
    gather_sem,
    part_sem,
    grad_sem,
    last_sem,
    local_sem,
):
    nx, nz, npl = sizes
    ng = nx * nz
    far = nz // 2
    g, p = lax.axis_index("grain"), lax.axis_index("plane")
    x, z = g // nz, lax.rem(g, nz)

    columns = [lax.rem(x + a, nx) * nz for a in range(nx)]

    def grain_peers(body):
        def far_row(m, carry):
            d = far + (1 - 2 * lax.rem(m, 2)) * ((m + 1) // 2)
            row = lax.rem(z + d, nz)
            for a in range(nx):
                body(m * nx + a, columns[a] + row)
            return carry

        lax.fori_loop(0, nz - 1, far_row, 0)
        for a in range(1, nx):
            body((nz - 1) * nx + a - 1, columns[a] + z)

    def plane_peer(i):
        return lax.rem(p + i + 1, npl)

    def each(n, body):
        def step(i, carry):
            body(i)
            return carry

        lax.fori_loop(0, n, step, 0)

    def to_grains(source, place, send_sem, recv_sem):
        def send(i, peer):
            pltpu.make_async_remote_copy(
                src_ref=source(peer),
                dst_ref=place(i),
                send_sem=send_sem,
                recv_sem=recv_sem,
                device_id=(peer, p),
                device_id_type=MESH,
            ).start()

        grain_peers(send)

    def to_planes(source, place, send_sem, recv_sem):
        def send(i):
            pltpu.make_async_remote_copy(
                src_ref=source,
                dst_ref=place(i),
                send_sem=send_sem,
                recv_sem=recv_sem,
                device_id=(g, plane_peer(i)),
                device_id_type=MESH,
            ).start()

        each(npl - 1, send)

    def wait(ref, sem):
        pltpu.make_async_copy(ref, ref, sem).wait()

    barrier = pltpu.get_barrier_semaphore()
    loads = [
        pltpu.make_async_copy(src, dst, local_sem.at[i])
        for i, (src, dst) in enumerate(
            [
                (block_grain_in, block_grain),
                (block_pixel_in, block_pixel),
                (block_count_in, block_count),
                (grains_in, grains),
                (pixels_in, pixels),
                (field_in, field),
            ]
        )
    ]
    for load in loads:
        load.start()
    grain_peers(lambda i, peer: pl.semaphore_signal(barrier, inc=1, device_id=(peer, p), device_id_type=MESH))
    each(
        npl - 1,
        lambda i: pl.semaphore_signal(barrier, inc=1, device_id=(g, plane_peer(i)), device_id_type=MESH),
    )
    for load in loads:
        load.wait()

    lane = lax.broadcasted_iota(jnp.int32, (8, 128), 1)

    def broadcast_lanes(tile):
        for r in range(96):
            c, b, k = r // 32, r // 8 % 4, r % 8
            spread[b, c, k] = jnp.broadcast_to(tile[:, r : r + 1], (8, 128))

    sub, col = (lax.broadcasted_iota(jnp.int32, (40, 128), i) for i in range(2))
    slot = jnp.where(col < 64, col, col - 64)
    row = lax.broadcasted_iota(jnp.int32, (1, 128), 1)
    edge = lax.broadcasted_iota(jnp.int32, (1, SLOTS), 1)
    count = block_count[...]

    def wide(value, fill):
        return jnp.concatenate([value, jnp.full((1, 128 - SLOTS), fill, jnp.int32)], axis=1)

    def upright(value):
        return jnp.sum(jnp.where(sub == col, value, 0), axis=1, keepdims=True)

    def over_slots(value):
        return jnp.sum(value, axis=0, keepdims=True)

    key = wide(jnp.where(edge < count, block_grain[...], 4), 5)
    key_up = upright(key)
    real = sub[:, 0:1] < SLOTS
    ahead = (key < key_up) | ((key == key_up) & (col < sub))
    rank = jnp.sum(ahead.astype(jnp.int32), axis=1, keepdims=True)
    place = (rank == slot) & real
    pixel = over_slots(jnp.where(place, upright(wide(block_pixel[...], 0)), 0))
    block = over_slots(jnp.where(place, key_up, 0))
    alive = over_slots(jnp.where(place & (key_up < 4), 1, 0))
    block = jnp.minimum(block, 3)
    below = over_slots(jnp.where((key_up < block) & real, 1, 0))
    same = jnp.where((row > 0) & ((row > below) | (alive == 0)), 1, 0)
    upto = over_slots(jnp.where((key_up <= row) & real, 1, 0))
    held = over_slots(jnp.where((key_up == row) & real, 1, 0))
    zero = jnp.zeros((1, 128), jnp.int32)
    table_made[...] = jnp.concatenate(
        [pixel, block, alive, same, jnp.maximum(upto - 1, 0), jnp.minimum(held, 1), zero, zero], axis=0
    )
    to_scalars = pltpu.make_async_copy(table_made, table, local_sem.at[6])
    to_scalars.start()
    target = jnp.where(alive > 0, 2 * pixel + jnp.where(row < 64, 0, 1), -1)
    picks[...] = (lax.broadcasted_iota(jnp.int32, (4 * ng, 128), 0) == target).astype(F32)

    grain_s = lax.broadcasted_iota(jnp.int32, (8, 256), 0) == lax.rem(lax.broadcasted_iota(jnp.int32, (8, 256), 1), 8)

    def product(a, b, over):
        return lax.dot_general(
            a, b, (((1,), (over,)), ((), ())), precision=lax.Precision.HIGHEST, preferred_element_type=F32
        )

    for c in range(3):
        eighth = lax.broadcasted_iota(jnp.int32, (256, 128), 0) // 8
        unfold[c] = (eighth + 32 * c == lax.broadcasted_iota(jnp.int32, (256, 128), 1)).astype(F32)

    def to_tile(value):
        return sum(product(jnp.where(grain_s, value[c : c + 1, :], 0.0), unfold[c], 0) for c in range(3))

    def from_tile(tile):
        parts = [jnp.sum(jnp.where(grain_s, product(tile, unfold[c], 1), 0.0), axis=0, keepdims=True) for c in range(3)]
        return jnp.concatenate(parts, axis=0)

    broadcast_lanes(to_tile(grains[...].astype(F32) * 0.03125))
    contrib[...] = jnp.zeros((128, 128), F32)

    for c in range(3):
        coords[c] = (pixels[c : c + 1, :].astype(F32) * 0.03125).reshape(4 * ng, 128)

    def make_sens(j):
        e, b = table[0, j], table[1, j]
        scale = table[2, j].astype(F32) * 27.0
        for h in range(2):
            px, py, pz = (coords[c, pl.ds(2 * e + h, 1), :] for c in range(3))
            for k in range(GROUPS):
                dx = px - spread[b, 0, k]
                dy = py - spread[b, 1, k]
                dz = pz - spread[b, 2, k]
                inv = lax.rsqrt(dx * dx + dy * dy + dz * dz)
                inv2 = inv * inv
                inv3 = inv2 * inv * scale
                along = 3.0 * dz * inv2 * inv3
                sens[j, 0, k, h] = along * dx
                sens[j, 1, k, h] = along * dy
                sens[j, 2, k, h] = along * dz - inv3

    def gather(it):
        to_grains(lambda peer: gather_send.at[it], lambda i: gathered.at[it, g], gather_sem.at[0, it], gather_sem.at[1, it])
        gathered[it, g] = gather_send[it]

    def gather_wait(it):
        wait(gathered.at[it, pl.ds(0, ng - 1)], gather_sem.at[1, it])

    def backward():
        def step(j, acc):
            e = table[0, j]
            keep = table[3, j].astype(F32)
            v0 = jnp.broadcast_to(rows[pl.ds(2 * e, 1), :], (8, 128))
            v1 = jnp.broadcast_to(rows[pl.ds(2 * e + 1, 1), :], (8, 128))
            out = []
            for c in range(3):
                for k in range(GROUPS):
                    i = c * GROUPS + k
                    t = acc[i] * keep + (sens[j, c, k, 0] * v0 + sens[j, c, k, 1] * v1)
                    snap[j, i] = t
                    out.append(t)
            return tuple(out)

        lax.fori_loop(0, SLOTS, step, tuple(jnp.zeros((8, 128), F32) for _ in range(24)))
        total = jnp.zeros((8, 128), F32)
        for b in range(4):
            last = table[4, b]
            held = table[5, b].astype(F32)
            for i in range(24):
                s = jnp.sum(snap[last, i], axis=1, keepdims=True) * held
                total = jnp.where(lane == (i // 8) * 32 + b * 8 + i % 8, s, total)
        return total

    def forward(it):
        def step(j, carry):
            b = table[1, j]
            acc = [[jnp.zeros((8, 128), F32) for _ in range(2)] for _ in range(2)]
            for c in range(3):
                for k in range(GROUPS):
                    d = spread[b, c, k]
                    for h in range(2):
                        acc[h][k % 2] = acc[h][k % 2] + sens[j, c, k, h] * d
            for h in range(2):
                contrib[pl.ds(64 * h + j, 1), :] = jnp.sum(acc[h][0] + acc[h][1], axis=0, keepdims=True)
            return carry

        lax.fori_loop(0, SLOTS, step, 0)
        part = jnp.dot(picks[...], contrib[...], precision=lax.Precision.HIGHEST, preferred_element_type=F32)
        part_send[it] = part.reshape(ng, 4, 128)
        to_grains(lambda peer: part_send.at[it, peer], lambda i: part_recv.at[it, i], part_sem.at[0, it], part_sem.at[1, it])
        wait(part_recv.at[it], part_sem.at[1, it])
        return jnp.sum(part_recv[it], axis=0) + part_send[it, g]

    def plane_sum(it, tile):
        grad_send[it] = tile
        to_planes(grad_send.at[it], lambda i: grad_recv.at[it, i], grad_sem.at[0, it], grad_sem.at[1, it])
        wait(grad_recv.at[it], grad_sem.at[1, it])
        return tile + jnp.sum(grad_recv[it], axis=0)

    def full_sum(tile):
        folded = jnp.sum(tile.reshape(-1, 4, 128), axis=0)
        return jnp.sum(jnp.sum(folded, axis=0, keepdims=True), axis=1, keepdims=True)

    to_scalars.wait()
    pl.semaphore_wait(barrier, ng - 1 + npl - 1)
    gather_send[0] = field[...]
    gather(0)
    each(SLOTS, make_sens)
    gather_wait(0)
    full_residual = gathered[0].reshape(4 * ng, 128)
    rows[...] = full_residual

    grad = plane_sum(0, backward())
    residual = field[...]
    moments = direction = pull = jnp.zeros((8, 128), F32)
    image = jnp.zeros((4, 128), F32)
    full_image = jnp.zeros((4 * ng, 128), F32)
    gamma = jnp.ones((1, 1), F32)
    delta = jnp.zeros((1, 1), F32)
    for it in range(ITERS):
        broadcast_lanes(grad)
        push = forward(it)
        if it + 1 < ITERS:
            gather_send[it + 1] = push
            gather(it + 1)
            gather_wait(it + 1)
            full = gathered[it + 1].reshape(4 * ng, 128)
            rows[...] = full
            sums = [full_sum(full_residual * full), full_sum(full * full)]
            if it > 0:
                sums.append(full_sum(full * full_image))
            tile = backward()
            for i, value in enumerate(sums):
                tile = jnp.where(lane == 96 + i, value, tile)
            tile = plane_sum(it + 1, tile)
            gamma_new, delta_new = tile[0:1, 96:97], tile[0:1, 97:98]
            tile_grad = jnp.where(lane >= 96, 0.0, tile)
            if it == 0:
                direction, pull, image, full_image, delta = grad, tile_grad, push, full, delta_new
            else:
                beta = gamma_new / gamma
                delta = delta_new + 2.0 * beta * tile[0:1, 98:99] + beta * beta * delta
                direction = grad + beta * direction
                pull = tile_grad + beta * pull
                image = push + beta * image
                full_image = full + beta * full_image
            gamma = gamma_new
            alpha = gamma / delta
            moments = moments + alpha * direction
            residual = residual - alpha * image
            full_residual = full_residual - alpha * full_image
            grad = grad - alpha * pull
        else:
            spot = lax.broadcasted_iota(jnp.int32, (1, 128), 1)
            sums = jnp.zeros((1, 128), F32)
            for i, other in enumerate((residual, push, image)):
                sums = jnp.where(spot == i, full_sum(push * other), sums)
            norm_send[...] = sums
            to_planes(norm_send, lambda i: norm_recv.at[i], last_sem.at[0], last_sem.at[1])
            moments_flat, direction_flat, grad_flat = from_tile(moments), from_tile(direction), from_tile(grad)
            wait(norm_recv, last_sem.at[1])
            sums = sums + jnp.sum(norm_recv[...], axis=0)
            total_send[...] = sums
            to_grains(lambda peer: total_send, lambda i: total_recv.at[i], last_sem.at[2], last_sem.at[3])
            wait(total_recv, last_sem.at[3])
            sums = sums + jnp.sum(total_recv[...], axis=0)
            beta = sums[:, 0:1] / gamma
            delta = sums[:, 1:2] + 2.0 * beta * sums[:, 2:3] + beta * beta * delta
            alpha = sums[:, 0:1] / delta
            moments_out[...] = moments_flat + alpha * (grad_flat + beta * direction_flat)
            residual_out[...] = residual - alpha * (push + beta * image)

    for it in range(ITERS):
        wait(gathered.at[it, pl.ds(0, ng - 1)], gather_sem.at[0, it])
        wait(part_recv.at[it], part_sem.at[0, it])
        wait(grad_recv.at[it], grad_sem.at[0, it])
    wait(norm_recv, last_sem.at[0])
    wait(total_recv, last_sem.at[2])


def local(sizes, field, grain_positions, pixel_coords, block_grain, block_pixel, block_count):
    nx, nz, npl = sizes
    ng = nx * nz
    vmem = pl.BlockSpec(memory_space=pltpu.VMEM)
    moments, residual = pl.pallas_call(
        functools.partial(kernel, sizes),
        out_shape=(jax.ShapeDtypeStruct((3, 256), F32), jax.ShapeDtypeStruct((4, 128), F32)),
        in_specs=[pl.BlockSpec(memory_space=pl.ANY)] * 6,
        out_specs=(vmem, vmem),
        scratch_shapes=[
            pltpu.VMEM((4, 128), F32),
            pltpu.VMEM((3, 256), jnp.int32),
            pltpu.VMEM((3, ng * 512), jnp.int32),
            pltpu.VMEM((1, SLOTS), jnp.int32),
            pltpu.VMEM((1, SLOTS), jnp.int32),
            pltpu.VMEM((1, 1), jnp.int32),
            pltpu.VMEM((8, 128), jnp.int32),
            pltpu.SMEM((8, 128), jnp.int32),
            pltpu.VMEM((3, 4 * ng, 128), F32),
            pltpu.VMEM((SLOTS, 3, GROUPS, 2, 8, 128), F32),
            pltpu.VMEM((4, 3, GROUPS, 8, 128), F32),
            pltpu.VMEM((SLOTS, 24, 8, 128), F32),
            pltpu.VMEM((4 * ng, 128), F32),
            pltpu.VMEM((3, 256, 128), F32),
            pltpu.VMEM((128, 128), F32),
            pltpu.VMEM((4 * ng, 128), F32),
            pltpu.VMEM((ITERS, 4, 128), F32),
            pltpu.VMEM((ITERS, ng, 4, 128), F32),
            pltpu.VMEM((ITERS, ng, 4, 128), F32),
            pltpu.VMEM((ITERS, ng - 1, 4, 128), F32),
            pltpu.VMEM((ITERS, 8, 128), F32),
            pltpu.VMEM((ITERS, npl - 1, 8, 128), F32),
            pltpu.VMEM((1, 128), F32),
            pltpu.VMEM((npl - 1, 1, 128), F32),
            pltpu.VMEM((1, 128), F32),
            pltpu.VMEM((ng - 1, 1, 128), F32),
            pltpu.SemaphoreType.DMA((2, ITERS)),
            pltpu.SemaphoreType.DMA((2, ITERS)),
            pltpu.SemaphoreType.DMA((2, ITERS)),
            pltpu.SemaphoreType.DMA((4,)),
            pltpu.SemaphoreType.DMA((7,)),
        ],
        compiler_params=pltpu.CompilerParams(collective_id=1, has_side_effects=True, vmem_limit_bytes=40 << 20),
        name="solve",
    )(field.reshape(4, 128), grain_positions, pixel_coords, block_grain, block_pixel, block_count)
    return moments, residual.reshape(512)


def solution(mesh, rows=4):
    grain, plane = mesh.shape["grain"], mesh.shape["plane"]
    placed = (
        P(("plane", "grain")),
        P(None, "grain"),
        P(None, "plane"),
        P("plane", "grain"),
        P("plane", "grain"),
        P("plane", "grain"),
    )
    return jax.shard_map(
        functools.partial(local, (rows, grain // rows, plane)),
        mesh=mesh,
        in_specs=placed,
        out_specs=(P(None, "grain"), P(("plane", "grain"))),
        check_vma=False,
    )
```

time: 122 us -> 114 us (0.934)
  Pallas kernels: 114 us -> 109 us
  local copies, waits for them, and re-layouts: 5.31 us -> 3.55 us
    pallas_call x1, Pallas kernels: 114 us -> 109 us  [local(): pl.pallas_call(functools.partial(kernel, sizes), out_shape=(jax.ShapeDtyp...]
    unnamed x11 -> x12, local copies, waits for them, and re-layouts: 4.17 us -> 3.55 us
where the time goes in v2:
time: 114 us
  Pallas kernels  109 us (96%)
  local copies, waits for them, and re-layouts  3.55 us (3%)
  between operations  1.33 us (1%)
    pallas_call x1, Pallas kernels, local(): pl.pallas_call(functools.partial(kernel, sizes), out_shape=(jax.ShapeDtyp...  109 us
    unnamed x12, local copies, waits for them, and re-layouts  3.55 us

profile of v2, /device:TPU:1, one launch (start us, length us, event | category | flops | bytes accessed | tf_op | source)
XLA Modules:
  0.0 114.0 jit_solution(13696144757168517640)
XLA Ops:
  0.6 0.0 copy-start.2
  1.3 0.0 copy-start.3
  1.3 0.0 copy-start.4
  1.3 0.0 copy-done.2
  1.3 0.6 copy-done.3
  2.0 0.0 copy-done.4
  2.0 0.0 copy-start
  2.0 1.0 copy-done
  3.0 0.0 copy-start.1
  3.0 0.7 copy-done.1
  3.7 109.2 %solve.1 = (f32[3,256]{1,0:T(4,128)S(1)}, f32[4,128]{1,0:T(4,128)S(1)}) custom-call(f32[4,128]{1,0:T(4,128)S(1)} %bitcast.2, s32[3,256]{1,0:T(4,128)S(1)} %copy-done.1, s32[3,32768]{1,0:T(4,128)S(1)} %copy-done, s32[1,36]{1,0:T(1,128)S(1)} %copy-done.3, s32[1,36]{1,0:T(1,128)S(1)} %copy-done.4, s32[1,1]{1,0:T(1,128)S(6)} %copy.10.block_count_in), custom_call_target="tpu_custom_call" | custom-call | tf_op jit(solution)/shard_map/solve/pallas_call | solution.py:372
  112.9 0.6 copy.11
  113.5 0.6 copy.12
Async XLA Ops:
  0.6 0.7 copy-start.2
  1.3 0.7 copy-start.3
  1.3 0.7 copy-start.4
  2.0 1.0 copy-start
  3.0 0.7 copy-start.1

commit v3 on v2

--- a/solution.py
+++ b/solution.py
@@ -11,6 +11,7 @@
 BLOCK_G = 64
 ITERS = 3
 SLOTS = 36
+UNROLL = 4
 GROUPS = 8
 F32 = jnp.float32
 
@@ -46,15 +47,18 @@
     part_send,
     part_recv,
     grad_send,
-    grad_recv,
+    grad_along,
+    grad_passed,
     norm_send,
-    norm_recv,
+    norm_along,
+    norm_passed,
     total_send,
     total_recv,
     gather_sem,
     part_sem,
     grad_sem,
     last_sem,
+    total_sem,
     local_sem,
 ):
     nx, nz, npl = sizes
@@ -62,23 +66,26 @@
     far = nz // 2
     g, p = lax.axis_index("grain"), lax.axis_index("plane")
     x, z = g // nz, lax.rem(g, nz)
+    ny = npl // 2
+    y, core = p // 2, lax.rem(p, 2)
 
     columns = [lax.rem(x + a, nx) * nz for a in range(nx)]
+    across = sorted(range(nx), key=lambda a: -min(a, nx - a))
 
     def grain_peers(body):
         def far_row(m, carry):
             d = far + (1 - 2 * lax.rem(m, 2)) * ((m + 1) // 2)
             row = lax.rem(z + d, nz)
-            for a in range(nx):
+            for a in across:
                 body(m * nx + a, columns[a] + row)
             return carry
 
         lax.fori_loop(0, nz - 1, far_row, 0)
-        for a in range(1, nx):
+        for a in across[:-1]:
             body((nz - 1) * nx + a - 1, columns[a] + z)
 
-    def plane_peer(i):
-        return lax.rem(p + i + 1, npl)
+    y_peers = [lax.rem(y + i, ny) * 2 + core for i in sorted(range(1, ny), key=lambda i: -min(i, ny - i))]
+    partner = p + 1 - 2 * core
 
     def each(n, body):
         def step(i, carry):
@@ -100,23 +107,39 @@
 
         grain_peers(send)
 
-    def to_planes(source, place, send_sem, recv_sem):
-        def send(i):
+    def plane_sum(value, sent, along, passed, sems):
+        sent[...] = value
+        for peer in y_peers:
             pltpu.make_async_remote_copy(
-                src_ref=source,
-                dst_ref=place(i),
-                send_sem=send_sem,
-                recv_sem=recv_sem,
-                device_id=(g, plane_peer(i)),
+                src_ref=sent,
+                dst_ref=along.at[y],
+                send_sem=sems.at[0],
+                recv_sem=sems.at[1],
+                device_id=(g, peer),
                 device_id_type=MESH,
             ).start()
-
-        each(npl - 1, send)
+        along[y] = value
+        wait(along.at[pl.ds(0, ny - 1)], sems.at[1])
+        value = jnp.sum(along[...], axis=0)
+        passed[0] = value
+        pltpu.make_async_remote_copy(
+            src_ref=passed.at[0],
+            dst_ref=passed.at[1],
+            send_sem=sems.at[2],
+            recv_sem=sems.at[3],
+            device_id=(g, partner),
+            device_id_type=MESH,
+        ).start()
+        wait(passed.at[1], sems.at[3])
+        return value + passed[1]
 
     def wait(ref, sem):
         pltpu.make_async_copy(ref, ref, sem).wait()
 
     barrier = pltpu.get_barrier_semaphore()
+    grain_peers(lambda i, peer: pl.semaphore_signal(barrier, inc=1, device_id=(peer, p), device_id_type=MESH))
+    for peer in (*y_peers, partner):
+        pl.semaphore_signal(barrier, inc=1, device_id=(g, peer), device_id_type=MESH)
     loads = [
         pltpu.make_async_copy(src, dst, local_sem.at[i])
         for i, (src, dst) in enumerate(
@@ -132,11 +155,6 @@
     ]
     for load in loads:
         load.start()
-    grain_peers(lambda i, peer: pl.semaphore_signal(barrier, inc=1, device_id=(peer, p), device_id_type=MESH))
-    each(
-        npl - 1,
-        lambda i: pl.semaphore_signal(barrier, inc=1, device_id=(g, plane_peer(i)), device_id_type=MESH),
-    )
     for load in loads:
         load.wait()
 
@@ -233,6 +251,14 @@
     def gather_wait(it):
         wait(gathered.at[it, pl.ds(0, ng - 1)], gather_sem.at[1, it])
 
+    def unrolled(step):
+        def several(i, carry):
+            for u in range(UNROLL):
+                carry = step(i * UNROLL + u, carry)
+            return carry
+
+        return several
+
     def backward():
         def step(j, acc):
             e = table[0, j]
@@ -248,7 +274,7 @@
                     out.append(t)
             return tuple(out)
 
-        lax.fori_loop(0, SLOTS, step, tuple(jnp.zeros((8, 128), F32) for _ in range(24)))
+        lax.fori_loop(0, SLOTS // UNROLL, unrolled(step), tuple(jnp.zeros((8, 128), F32) for _ in range(24)))
         total = jnp.zeros((8, 128), F32)
         for b in range(4):
             last = table[4, b]
@@ -271,25 +297,24 @@
                 contrib[pl.ds(64 * h + j, 1), :] = jnp.sum(acc[h][0] + acc[h][1], axis=0, keepdims=True)
             return carry
 
-        lax.fori_loop(0, SLOTS, step, 0)
+        lax.fori_loop(0, SLOTS // UNROLL, unrolled(step), 0)
         part = jnp.dot(picks[...], contrib[...], precision=lax.Precision.HIGHEST, preferred_element_type=F32)
         part_send[it] = part.reshape(ng, 4, 128)
         to_grains(lambda peer: part_send.at[it, peer], lambda i: part_recv.at[it, i], part_sem.at[0, it], part_sem.at[1, it])
         wait(part_recv.at[it], part_sem.at[1, it])
         return jnp.sum(part_recv[it], axis=0) + part_send[it, g]
 
-    def plane_sum(it, tile):
-        grad_send[it] = tile
-        to_planes(grad_send.at[it], lambda i: grad_recv.at[it, i], grad_sem.at[0, it], grad_sem.at[1, it])
-        wait(grad_recv.at[it], grad_sem.at[1, it])
-        return tile + jnp.sum(grad_recv[it], axis=0)
-
-    def full_sum(tile):
-        folded = jnp.sum(tile.reshape(-1, 4, 128), axis=0)
-        return jnp.sum(jnp.sum(folded, axis=0, keepdims=True), axis=1, keepdims=True)
+    def grad_sum(it, tile):
+        return plane_sum(tile, grad_send.at[it], grad_along.at[it], grad_passed.at[it], grad_sem.at[it])
+
+    def column(value):
+        return jnp.sum(jnp.sum(value.reshape(-1, 8, 128), axis=0), axis=1, keepdims=True)
+
+    def full_sum(value):
+        return jnp.sum(jnp.sum(value, axis=0, keepdims=True), axis=1, keepdims=True)
 
     to_scalars.wait()
-    pl.semaphore_wait(barrier, ng - 1 + npl - 1)
+    pl.semaphore_wait(barrier, ng - 1 + ny)
     gather_send[0] = field[...]
     gather(0)
     each(SLOTS, make_sens)
@@ -297,7 +322,7 @@
     full_residual = gathered[0].reshape(4 * ng, 128)
     rows[...] = full_residual
 
-    grad = plane_sum(0, backward())
+    grad = grad_sum(0, backward())
     residual = field[...]
     moments = direction = pull = jnp.zeros((8, 128), F32)
     image = jnp.zeros((4, 128), F32)
@@ -313,20 +338,21 @@
             gather_wait(it + 1)
             full = gathered[it + 1].reshape(4 * ng, 128)
             rows[...] = full
-            sums = [full_sum(full_residual * full), full_sum(full * full)]
+            sums = [column(full_residual * full), column(full * full)]
             if it > 0:
-                sums.append(full_sum(full * full_image))
+                sums.append(column(full * full_image))
             tile = backward()
             for i, value in enumerate(sums):
                 tile = jnp.where(lane == 96 + i, value, tile)
-            tile = plane_sum(it + 1, tile)
-            gamma_new, delta_new = tile[0:1, 96:97], tile[0:1, 97:98]
+            tile = grad_sum(it + 1, tile)
+            totals = jnp.sum(tile, axis=0, keepdims=True)
+            gamma_new, delta_new = totals[:, 96:97], totals[:, 97:98]
             tile_grad = jnp.where(lane >= 96, 0.0, tile)
             if it == 0:
                 direction, pull, image, full_image, delta = grad, tile_grad, push, full, delta_new
             else:
                 beta = gamma_new / gamma
-                delta = delta_new + 2.0 * beta * tile[0:1, 98:99] + beta * beta * delta
+                delta = delta_new + 2.0 * beta * totals[:, 98:99] + beta * beta * delta
                 direction = grad + beta * direction
                 pull = tile_grad + beta * pull
                 image = push + beta * image
@@ -342,15 +368,13 @@
             sums = jnp.zeros((1, 128), F32)
             for i, other in enumerate((residual, push, image)):
                 sums = jnp.where(spot == i, full_sum(push * other), sums)
-            norm_send[...] = sums
-            to_planes(norm_send, lambda i: norm_recv.at[i], last_sem.at[0], last_sem.at[1])
             moments_flat, direction_flat, grad_flat = from_tile(moments), from_tile(direction), from_tile(grad)
-            wait(norm_recv, last_sem.at[1])
-            sums = sums + jnp.sum(norm_recv[...], axis=0)
+            sums = plane_sum(sums, norm_send, norm_along, norm_passed, last_sem)
             total_send[...] = sums
-            to_grains(lambda peer: total_send, lambda i: total_recv.at[i], last_sem.at[2], last_sem.at[3])
-            wait(total_recv, last_sem.at[3])
-            sums = sums + jnp.sum(total_recv[...], axis=0)
+            total_recv[g] = sums
+            to_grains(lambda peer: total_send, lambda i: total_recv.at[g], total_sem.at[0], total_sem.at[1])
+            wait(total_recv.at[pl.ds(0, ng - 1)], total_sem.at[1])
+            sums = jnp.sum(total_recv[...], axis=0)
             beta = sums[:, 0:1] / gamma
             delta = sums[:, 1:2] + 2.0 * beta * sums[:, 2:3] + beta * beta * delta
             alpha = sums[:, 0:1] / delta
@@ -360,9 +384,11 @@
     for it in range(ITERS):
         wait(gathered.at[it, pl.ds(0, ng - 1)], gather_sem.at[0, it])
         wait(part_recv.at[it], part_sem.at[0, it])
-        wait(grad_recv.at[it], grad_sem.at[0, it])
-    wait(norm_recv, last_sem.at[0])
-    wait(total_recv, last_sem.at[2])
+        wait(grad_along.at[it, pl.ds(0, ny - 1)], grad_sem.at[it, 0])
+        wait(grad_passed.at[it, 0], grad_sem.at[it, 2])
+    wait(norm_along.at[pl.ds(0, ny - 1)], last_sem.at[0])
+    wait(norm_passed.at[0], last_sem.at[2])
+    wait(total_recv.at[pl.ds(0, ng - 1)], total_sem.at[0])
 
 
 def local(sizes, field, grain_positions, pixel_coords, block_grain, block_pixel, block_count):
@@ -372,7 +398,7 @@
     moments, residual = pl.pallas_call(
         functools.partial(kernel, sizes),
         out_shape=(jax.ShapeDtypeStruct((3, 256), F32), jax.ShapeDtypeStruct((4, 128), F32)),
-        in_specs=[pl.BlockSpec(memory_space=pl.ANY)] * 6,
+        in_specs=[pl.BlockSpec(memory_space=pltpu.HBM)] * 6,
         out_specs=(vmem, vmem),
         scratch_shapes=[
             pltpu.VMEM((4, 128), F32),
@@ -396,18 +422,21 @@
             pltpu.VMEM((ITERS, ng, 4, 128), F32),
             pltpu.VMEM((ITERS, ng - 1, 4, 128), F32),
             pltpu.VMEM((ITERS, 8, 128), F32),
-            pltpu.VMEM((ITERS, npl - 1, 8, 128), F32),
+            pltpu.VMEM((ITERS, npl // 2, 8, 128), F32),
+            pltpu.VMEM((ITERS, 2, 8, 128), F32),
             pltpu.VMEM((1, 128), F32),
-            pltpu.VMEM((npl - 1, 1, 128), F32),
+            pltpu.VMEM((npl // 2, 1, 128), F32),
+            pltpu.VMEM((2, 1, 128), F32),
             pltpu.VMEM((1, 128), F32),
-            pltpu.VMEM((ng - 1, 1, 128), F32),
+            pltpu.VMEM((ng, 1, 128), F32),
             pltpu.SemaphoreType.DMA((2, ITERS)),
             pltpu.SemaphoreType.DMA((2, ITERS)),
-            pltpu.SemaphoreType.DMA((2, ITERS)),
+            pltpu.SemaphoreType.DMA((ITERS, 4)),
             pltpu.SemaphoreType.DMA((4,)),
+            pltpu.SemaphoreType.DMA((2,)),
             pltpu.SemaphoreType.DMA((7,)),
         ],
-        compiler_params=pltpu.CompilerParams(collective_id=1, has_side_effects=True, vmem_limit_bytes=40 << 20),
+        compiler_params=pltpu.CompilerParams(collective_id=1, has_side_effects=True, vmem_limit_bytes=60 << 20),
         name="solve",
     )(field.reshape(4, 128), grain_positions, pixel_coords, block_grain, block_pixel, block_count)
     return moments, residual.reshape(512)

time: 114 us -> 112 us (0.982)
  local copies, waits for them, and re-layouts: 3.55 us -> 1.91 us
    unnamed x12 -> x6, local copies, waits for them, and re-layouts: 3.55 us -> 1.91 us
where the time goes in v3:
time: 112 us
  Pallas kernels  109 us (97%)
  local copies, waits for them, and re-layouts  1.91 us (2%)
  between operations  1.3 us (1%)
    pallas_call x1, Pallas kernels, local(): pl.pallas_call(functools.partial(kernel, sizes), out_shape=(jax.ShapeDtyp...  109 us

profile of v3, /device:TPU:1, one launch (start us, length us, event | category | flops | bytes accessed | tf_op | source)
XLA Modules:
  0.0 112.3 jit_solution(1776471952726009096)
XLA Ops:
  1.3 109.1 %solve.1 = (f32[3,256]{1,0:T(4,128)}, f32[4,128]{1,0:T(4,128)}) custom-call(f32[4,128]{1,0:T(4,128)} %bitcast.2, s32[3,256]{1,0:T(4,128)} %grains_in.1, s32[3,32768]{1,0:T(4,128)} %pixels_in.1, s32[1,36]{1,0:T(1,128)} %block_grain_in.1, s32[1,36]{1,0:T(1,128)} %block_pixel_in.1, s32[1,1]{1,0:T(1,128)S(6)} %copy.10.block_count_in), custom_call_target="tpu_custom_call" | custom-call | tf_op jit(solution)/shard_map/solve/pallas_call | solution.py:398
  110.4 0.0 copy-start
  110.4 0.7 copy-done
  111.1 0.0 copy-start.1
  111.1 0.6 copy.11
  111.6 0.1 copy-done.1
  111.7 0.6 copy.12
Async XLA Ops:
  110.4 0.7 copy-start
  111.1 0.7 copy-start.1

commit v4 on v3

--- a/solution.py
+++ b/solution.py
@@ -11,7 +11,7 @@
 BLOCK_G = 64
 ITERS = 3
 SLOTS = 36
-UNROLL = 4
+UNROLL = 6
 GROUPS = 8
 F32 = jnp.float32
 
@@ -42,16 +42,16 @@
     unfold,
     contrib,
     rows,
+    full_residual,
+    full_image,
     gather_send,
     gathered,
     part_send,
     part_recv,
     grad_send,
-    grad_along,
-    grad_passed,
+    grad_recv,
     norm_send,
-    norm_along,
-    norm_passed,
+    norm_recv,
     total_send,
     total_recv,
     gather_sem,
@@ -66,8 +66,6 @@
     far = nz // 2
     g, p = lax.axis_index("grain"), lax.axis_index("plane")
     x, z = g // nz, lax.rem(g, nz)
-    ny = npl // 2
-    y, core = p // 2, lax.rem(p, 2)
 
     columns = [lax.rem(x + a, nx) * nz for a in range(nx)]
     across = sorted(range(nx), key=lambda a: -min(a, nx - a))
@@ -84,8 +82,9 @@
         for a in across[:-1]:
             body((nz - 1) * nx + a - 1, columns[a] + z)
 
-    y_peers = [lax.rem(y + i, ny) * 2 + core for i in sorted(range(1, ny), key=lambda i: -min(i, ny - i))]
-    partner = p + 1 - 2 * core
+    def plane_peers(body):
+        for i in range(1, npl):
+            body(lax.rem(p + i, npl))
 
     def each(n, body):
         def step(i, carry):
@@ -107,39 +106,30 @@
 
         grain_peers(send)
 
-    def plane_sum(value, sent, along, passed, sems):
+    def plane_sum(value, sent, landed, sems):
         sent[...] = value
-        for peer in y_peers:
+
+        def send(peer):
             pltpu.make_async_remote_copy(
                 src_ref=sent,
-                dst_ref=along.at[y],
+                dst_ref=landed.at[p],
                 send_sem=sems.at[0],
                 recv_sem=sems.at[1],
                 device_id=(g, peer),
                 device_id_type=MESH,
             ).start()
-        along[y] = value
-        wait(along.at[pl.ds(0, ny - 1)], sems.at[1])
-        value = jnp.sum(along[...], axis=0)
-        passed[0] = value
-        pltpu.make_async_remote_copy(
-            src_ref=passed.at[0],
-            dst_ref=passed.at[1],
-            send_sem=sems.at[2],
-            recv_sem=sems.at[3],
-            device_id=(g, partner),
-            device_id_type=MESH,
-        ).start()
-        wait(passed.at[1], sems.at[3])
-        return value + passed[1]
+
+        plane_peers(send)
+        landed[p] = value
+        wait(landed.at[pl.ds(0, npl - 1)], sems.at[1])
+        return jnp.sum(landed[...], axis=0)
 
     def wait(ref, sem):
         pltpu.make_async_copy(ref, ref, sem).wait()
 
     barrier = pltpu.get_barrier_semaphore()
     grain_peers(lambda i, peer: pl.semaphore_signal(barrier, inc=1, device_id=(peer, p), device_id_type=MESH))
-    for peer in (*y_peers, partner):
-        pl.semaphore_signal(barrier, inc=1, device_id=(g, peer), device_id_type=MESH)
+    plane_peers(lambda peer: pl.semaphore_signal(barrier, inc=1, device_id=(g, peer), device_id_type=MESH))
     loads = [
         pltpu.make_async_copy(src, dst, local_sem.at[i])
         for i, (src, dst) in enumerate(
@@ -201,7 +191,9 @@
     to_scalars = pltpu.make_async_copy(table_made, table, local_sem.at[6])
     to_scalars.start()
     target = jnp.where(alive > 0, 2 * pixel + jnp.where(row < 64, 0, 1), -1)
-    picks[...] = (lax.broadcasted_iota(jnp.int32, (4 * ng, 128), 0) == target).astype(F32)
+    chosen = (lax.broadcasted_iota(jnp.int32, (4 * ng, 128), 0) == target).astype(F32).astype(jnp.bfloat16)
+    for i in range(3):
+        picks[:, 128 * i : 128 * (i + 1)] = chosen
 
     grain_s = lax.broadcasted_iota(jnp.int32, (8, 256), 0) == lax.rem(lax.broadcasted_iota(jnp.int32, (8, 256), 1), 8)
 
@@ -284,7 +276,7 @@
                 total = jnp.where(lane == (i // 8) * 32 + b * 8 + i % 8, s, total)
         return total
 
-    def forward(it):
+    def forward(it, meanwhile):
         def step(j, carry):
             b = table[1, j]
             acc = [[jnp.zeros((8, 128), F32) for _ in range(2)] for _ in range(2)]
@@ -298,14 +290,21 @@
             return carry
 
         lax.fori_loop(0, SLOTS // UNROLL, unrolled(step), 0)
-        part = jnp.dot(picks[...], contrib[...], precision=lax.Precision.HIGHEST, preferred_element_type=F32)
+        value = contrib[...]
+        high = value.astype(jnp.bfloat16)
+        rest = value - high.astype(F32)
+        middle = rest.astype(jnp.bfloat16)
+        low = (rest - middle.astype(F32)).astype(jnp.bfloat16)
+        pieces = jnp.concatenate([high, middle, low], axis=0)
+        part = jnp.dot(picks[...], pieces, preferred_element_type=F32)
         part_send[it] = part.reshape(ng, 4, 128)
         to_grains(lambda peer: part_send.at[it, peer], lambda i: part_recv.at[it, i], part_sem.at[0, it], part_sem.at[1, it])
+        meanwhile()
         wait(part_recv.at[it], part_sem.at[1, it])
         return jnp.sum(part_recv[it], axis=0) + part_send[it, g]
 
     def grad_sum(it, tile):
-        return plane_sum(tile, grad_send.at[it], grad_along.at[it], grad_passed.at[it], grad_sem.at[it])
+        return plane_sum(tile, grad_send.at[it], grad_recv.at[it], grad_sem.at[it])
 
     def column(value):
         return jnp.sum(jnp.sum(value.reshape(-1, 8, 128), axis=0), axis=1, keepdims=True)
@@ -314,65 +313,63 @@
         return jnp.sum(jnp.sum(value, axis=0, keepdims=True), axis=1, keepdims=True)
 
     to_scalars.wait()
-    pl.semaphore_wait(barrier, ng - 1 + ny)
+    pl.semaphore_wait(barrier, ng - 1 + npl - 1)
     gather_send[0] = field[...]
     gather(0)
     each(SLOTS, make_sens)
     gather_wait(0)
-    full_residual = gathered[0].reshape(4 * ng, 128)
-    rows[...] = full_residual
+    rows[...] = gathered[0].reshape(4 * ng, 128)
+    full_residual[...] = rows[...]
 
     grad = grad_sum(0, backward())
     residual = field[...]
     moments = direction = pull = jnp.zeros((8, 128), F32)
     image = jnp.zeros((4, 128), F32)
-    full_image = jnp.zeros((4 * ng, 128), F32)
     gamma = jnp.ones((1, 1), F32)
-    delta = jnp.zeros((1, 1), F32)
+    alpha = beta = delta = jnp.zeros((1, 1), F32)
+    full_image[...] = jnp.zeros((4 * ng, 128), F32)
     for it in range(ITERS):
         broadcast_lanes(grad)
-        push = forward(it)
+
+        def meanwhile():
+            if 0 < it < ITERS - 1:
+                full_image[...] = rows[...] + beta * full_image[...]
+                full_residual[...] = full_residual[...] - alpha * full_image[...]
+
+        push = forward(it, meanwhile)
         if it + 1 < ITERS:
             gather_send[it + 1] = push
             gather(it + 1)
             gather_wait(it + 1)
             full = gathered[it + 1].reshape(4 * ng, 128)
             rows[...] = full
-            sums = [column(full_residual * full), column(full * full)]
-            if it > 0:
-                sums.append(column(full * full_image))
+            sums = [column(full_residual[...] * full), column(full * full), column(full * full_image[...])]
             tile = backward()
             for i, value in enumerate(sums):
                 tile = jnp.where(lane == 96 + i, value, tile)
             tile = grad_sum(it + 1, tile)
             totals = jnp.sum(tile, axis=0, keepdims=True)
-            gamma_new, delta_new = totals[:, 96:97], totals[:, 97:98]
-            tile_grad = jnp.where(lane >= 96, 0.0, tile)
-            if it == 0:
-                direction, pull, image, full_image, delta = grad, tile_grad, push, full, delta_new
-            else:
-                beta = gamma_new / gamma
-                delta = delta_new + 2.0 * beta * totals[:, 98:99] + beta * beta * delta
-                direction = grad + beta * direction
-                pull = tile_grad + beta * pull
-                image = push + beta * image
-                full_image = full + beta * full_image
+            gamma_new = totals[:, 96:97]
+            beta = gamma_new / gamma if it > 0 else jnp.zeros((1, 1), F32)
+            delta = totals[:, 97:98] + 2.0 * beta * totals[:, 98:99] + beta * beta * delta
             gamma = gamma_new
             alpha = gamma / delta
+            pull = jnp.where(lane >= 96, 0.0, tile) + beta * pull
+            direction = grad + beta * direction
             moments = moments + alpha * direction
+            image = push + beta * image
             residual = residual - alpha * image
-            full_residual = full_residual - alpha * full_image
             grad = grad - alpha * pull
         else:
             spot = lax.broadcasted_iota(jnp.int32, (1, 128), 1)
             sums = jnp.zeros((1, 128), F32)
             for i, other in enumerate((residual, push, image)):
                 sums = jnp.where(spot == i, full_sum(push * other), sums)
-            moments_flat, direction_flat, grad_flat = from_tile(moments), from_tile(direction), from_tile(grad)
-            sums = plane_sum(sums, norm_send, norm_along, norm_passed, last_sem)
+            sums = plane_sum(sums, norm_send, norm_recv, last_sem)
             total_send[...] = sums
             total_recv[g] = sums
             to_grains(lambda peer: total_send, lambda i: total_recv.at[g], total_sem.at[0], total_sem.at[1])
+            moments_flat, direction_flat, grad_flat = from_tile(moments), from_tile(direction), from_tile(grad)
             wait(total_recv.at[pl.ds(0, ng - 1)], total_sem.at[1])
             sums = jnp.sum(total_recv[...], axis=0)
             beta = sums[:, 0:1] / gamma
@@ -384,10 +381,8 @@
     for it in range(ITERS):
         wait(gathered.at[it, pl.ds(0, ng - 1)], gather_sem.at[0, it])
         wait(part_recv.at[it], part_sem.at[0, it])
-        wait(grad_along.at[it, pl.ds(0, ny - 1)], grad_sem.at[it, 0])
-        wait(grad_passed.at[it, 0], grad_sem.at[it, 2])
-    wait(norm_along.at[pl.ds(0, ny - 1)], last_sem.at[0])
-    wait(norm_passed.at[0], last_sem.at[2])
+        wait(grad_recv.at[it, pl.ds(0, npl - 1)], grad_sem.at[it, 0])
+    wait(norm_recv.at[pl.ds(0, npl - 1)], last_sem.at[0])
     wait(total_recv.at[pl.ds(0, ng - 1)], total_sem.at[0])
 
 
@@ -413,26 +408,26 @@
             pltpu.VMEM((SLOTS, 3, GROUPS, 2, 8, 128), F32),
             pltpu.VMEM((4, 3, GROUPS, 8, 128), F32),
             pltpu.VMEM((SLOTS, 24, 8, 128), F32),
-            pltpu.VMEM((4 * ng, 128), F32),
+            pltpu.VMEM((4 * ng, 384), jnp.bfloat16),
             pltpu.VMEM((3, 256, 128), F32),
             pltpu.VMEM((128, 128), F32),
+            pltpu.VMEM((4 * ng, 128), F32),
+            pltpu.VMEM((4 * ng, 128), F32),
             pltpu.VMEM((4 * ng, 128), F32),
             pltpu.VMEM((ITERS, 4, 128), F32),
             pltpu.VMEM((ITERS, ng, 4, 128), F32),
             pltpu.VMEM((ITERS, ng, 4, 128), F32),
             pltpu.VMEM((ITERS, ng - 1, 4, 128), F32),
             pltpu.VMEM((ITERS, 8, 128), F32),
-            pltpu.VMEM((ITERS, npl // 2, 8, 128), F32),
-            pltpu.VMEM((ITERS, 2, 8, 128), F32),
+            pltpu.VMEM((ITERS, npl, 8, 128), F32),
             pltpu.VMEM((1, 128), F32),
-            pltpu.VMEM((npl // 2, 1, 128), F32),
-            pltpu.VMEM((2, 1, 128), F32),
+            pltpu.VMEM((npl, 1, 128), F32),
             pltpu.VMEM((1, 128), F32),
             pltpu.VMEM((ng, 1, 128), F32),
             pltpu.SemaphoreType.DMA((2, ITERS)),
             pltpu.SemaphoreType.DMA((2, ITERS)),
-            pltpu.SemaphoreType.DMA((ITERS, 4)),
-            pltpu.SemaphoreType.DMA((4,)),
+            pltpu.SemaphoreType.DMA((ITERS, 2)),
+            pltpu.SemaphoreType.DMA((2,)),
             pltpu.SemaphoreType.DMA((2,)),
             pltpu.SemaphoreType.DMA((7,)),
         ],

time: 112 us -> 109 us (0.973)
  Pallas kernels: 109 us -> 106 us
    pallas_call x1, Pallas kernels: 109 us -> 106 us  [local(): pl.pallas_call(functools.partial(kernel, sizes), out_shape=(jax.ShapeDtyp...]
where the time goes in v4:
time: 109 us
  Pallas kernels  106 us (97%)
  local copies, waits for them, and re-layouts  1.91 us (2%)
  between operations  1.3 us (1%)
    pallas_call x1, Pallas kernels, local(): pl.pallas_call(functools.partial(kernel, sizes), out_shape=(jax.ShapeDtyp...  106 us

profile of v4, /device:TPU:1, one launch (start us, length us, event | category | flops | bytes accessed | tf_op | source)
XLA Modules:
  0.0 109.0 jit_solution(14433930474037475044)
XLA Ops:
  1.3 105.8 %solve.1 = (f32[3,256]{1,0:T(4,128)}, f32[4,128]{1,0:T(4,128)}) custom-call(f32[4,128]{1,0:T(4,128)} %bitcast.2, s32[3,256]{1,0:T(4,128)} %grains_in.1, s32[3,32768]{1,0:T(4,128)} %pixels_in.1, s32[1,36]{1,0:T(1,128)} %block_grain_in.1, s32[1,36]{1,0:T(1,128)} %block_pixel_in.1, s32[1,1]{1,0:T(1,128)S(6)} %copy.10.block_count_in), custom_call_target="tpu_custom_call" | custom-call | tf_op jit(solution)/shard_map/solve/pallas_call | solution.py:393
  107.1 0.0 copy-start
  107.1 0.7 copy-done
  107.8 0.0 copy-start.1
  107.8 0.6 copy.11
  108.4 0.1 copy-done.1
  108.4 0.6 copy.12
Async XLA Ops:
  107.1 0.7 copy-start
  107.8 0.7 copy-start.1

commit v5 on v4

--- a/solution.py
+++ b/solution.py
@@ -243,6 +243,11 @@
     def gather_wait(it):
         wait(gathered.at[it, pl.ds(0, ng - 1)], gather_sem.at[1, it])
 
+    def pairwise(values):
+        while len(values) > 1:
+            values = [sum(values[i : i + 2]) for i in range(0, len(values), 2)]
+        return values[0]
+
     def unrolled(step):
         def several(i, carry):
             for u in range(UNROLL):
@@ -267,14 +272,17 @@
             return tuple(out)
 
         lax.fori_loop(0, SLOTS // UNROLL, unrolled(step), tuple(jnp.zeros((8, 128), F32) for _ in range(24)))
-        total = jnp.zeros((8, 128), F32)
+        totals = []
         for b in range(4):
             last = table[4, b]
             held = table[5, b].astype(F32)
-            for i in range(24):
-                s = jnp.sum(snap[last, i], axis=1, keepdims=True) * held
-                total = jnp.where(lane == (i // 8) * 32 + b * 8 + i % 8, s, total)
-        return total
+            for c in range(3):
+                part = jnp.zeros((8, 128), F32)
+                for k in range(GROUPS):
+                    s = jnp.sum(snap[last, c * GROUPS + k], axis=1, keepdims=True)
+                    part = jnp.where(lane == c * 32 + b * 8 + k, s, part)
+                totals.append(part * held)
+        return pairwise(totals)
 
     def forward(it, meanwhile):
         def step(j, carry):
@@ -301,7 +309,8 @@
         to_grains(lambda peer: part_send.at[it, peer], lambda i: part_recv.at[it, i], part_sem.at[0, it], part_sem.at[1, it])
         meanwhile()
         wait(part_recv.at[it], part_sem.at[1, it])
-        return jnp.sum(part_recv[it], axis=0) + part_send[it, g]
+        chains = [jnp.sum(part_recv[it, i : min(i + 8, ng - 1)], axis=0) for i in range(0, ng - 1, 8)]
+        return pairwise(chains) + part_send[it, g]
 
     def grad_sum(it, tile):
         return plane_sum(tile, grad_send.at[it], grad_recv.at[it], grad_sem.at[it])
@@ -313,8 +322,8 @@
         return jnp.sum(jnp.sum(value, axis=0, keepdims=True), axis=1, keepdims=True)
 
     to_scalars.wait()
+    gather_send[0] = field[...]
     pl.semaphore_wait(barrier, ng - 1 + npl - 1)
-    gather_send[0] = field[...]
     gather(0)
     each(SLOTS, make_sens)
     gather_wait(0)
@@ -371,7 +380,7 @@
             to_grains(lambda peer: total_send, lambda i: total_recv.at[g], total_sem.at[0], total_sem.at[1])
             moments_flat, direction_flat, grad_flat = from_tile(moments), from_tile(direction), from_tile(grad)
             wait(total_recv.at[pl.ds(0, ng - 1)], total_sem.at[1])
-            sums = jnp.sum(total_recv[...], axis=0)
+            sums = pairwise([jnp.sum(total_recv[i : i + 8], axis=0) for i in range(0, ng, 8)])
             beta = sums[:, 0:1] / gamma
             delta = sums[:, 1:2] + 2.0 * beta * sums[:, 2:3] + beta * beta * delta
             alpha = sums[:, 0:1] / delta
@@ -384,6 +393,17 @@
         wait(grad_recv.at[it, pl.ds(0, npl - 1)], grad_sem.at[it, 0])
     wait(norm_recv.at[pl.ds(0, npl - 1)], last_sem.at[0])
     wait(total_recv.at[pl.ds(0, ng - 1)], total_sem.at[0])
+
+
+def hand_on(moments, residual, moments_out, residual_out, sems):
+    copies = [
+        pltpu.make_async_copy(moments, moments_out, sems.at[0]),
+        pltpu.make_async_copy(residual, residual_out, sems.at[1]),
+    ]
+    for copy in copies:
+        copy.start()
+    for copy in copies:
+        copy.wait()
 
 
 def local(sizes, field, grain_positions, pixel_coords, block_grain, block_pixel, block_count):
@@ -434,6 +454,16 @@
         compiler_params=pltpu.CompilerParams(collective_id=1, has_side_effects=True, vmem_limit_bytes=60 << 20),
         name="solve",
     )(field.reshape(4, 128), grain_positions, pixel_coords, block_grain, block_pixel, block_count)
+    held = pl.BlockSpec(memory_space=pltpu.HBM)
+    moments, residual = pl.pallas_call(
+        hand_on,
+        out_shape=(jax.ShapeDtypeStruct((3, 256), F32), jax.ShapeDtypeStruct((4, 128), F32)),
+        in_specs=[held] * 2,
+        out_specs=(held, held),
+        scratch_shapes=[pltpu.SemaphoreType.DMA((2,))],
+        compiler_params=pltpu.CompilerParams(vmem_limit_bytes=60 << 20),
+        name="hand_on",
+    )(moments, residual)
     return moments, residual.reshape(512)
 
 

time: 109 us -> 108 us (level)
  local copies, waits for them, and re-layouts: 1.91 us -> 0 us
    unnamed x6 -> x0, local copies, waits for them, and re-layouts: 1.91 us -> none
    pallas_call x0 -> x1, Pallas kernels: none -> 1.31 us  [local(): pl.pallas_call(hand_on, out_shape=(jax.ShapeDtypeStruct((3, 256), F32), j...]
where the time goes in v5:
time: 108 us
  Pallas kernels  106 us (98%)
  between operations  1.29 us (1%)
    pallas_call x1, Pallas kernels, local(): pl.pallas_call(functools.partial(kernel, sizes), out_shape=(jax.ShapeDtyp...  105 us

profile of v5, /device:TPU:1, one launch (start us, length us, event | category | flops | bytes accessed | tf_op | source)
XLA Modules:
  0.0 107.6 jit_solution(9719653869728434924)
XLA Ops:
  1.3 105.0 %solve.1 = (f32[3,256]{1,0:T(4,128)}, f32[4,128]{1,0:T(4,128)}) custom-call(f32[4,128]{1,0:T(4,128)} %bitcast.2, s32[3,256]{1,0:T(4,128)} %grains_in.1, s32[3,32768]{1,0:T(4,128)} %pixels_in.1, s32[1,36]{1,0:T(1,128)} %block_grain_in.1, s32[1,36]{1,0:T(1,128)} %block_pixel_in.1, s32[1,1]{1,0:T(1,128)S(6)} %copy.8.block_count_in), custom_call_target="tpu_custom_call" | custom-call | tf_op jit(solution)/shard_map/solve/pallas_call | solution.py:413
  106.3 1.3 %hand_on.1 = (f32[3,256]{1,0:T(4,128)}, f32[4,128]{1,0:T(4,128)}) custom-call(f32[3,256]{1,0:T(4,128)} %get-tuple-element.6.moments, f32[4,128]{1,0:T(4,128)} %get-tuple-element.7.residual), custom_call_target="tpu_custom_call" | custom-call | tf_op jit(solution)/shard_map/hand_on/pallas_call | solution.py:458

commit v6 on v5

--- a/solution.py
+++ b/solution.py
@@ -451,17 +451,23 @@
             pltpu.SemaphoreType.DMA((2,)),
             pltpu.SemaphoreType.DMA((7,)),
         ],
-        compiler_params=pltpu.CompilerParams(collective_id=1, has_side_effects=True, vmem_limit_bytes=60 << 20),
+        compiler_params=pltpu.CompilerParams(collective_id=1, has_side_effects=True, vmem_limit_bytes=40 << 20),
         name="solve",
-    )(field.reshape(4, 128), grain_positions, pixel_coords, block_grain, block_pixel, block_count)
+    )(
+        *(
+            pltpu.with_memory_space_constraint(value, pltpu.HBM)
+            for value in (field.reshape(4, 128), grain_positions, pixel_coords, block_grain, block_pixel)
+        ),
+        block_count,
+    )
     held = pl.BlockSpec(memory_space=pltpu.HBM)
     moments, residual = pl.pallas_call(
         hand_on,
         out_shape=(jax.ShapeDtypeStruct((3, 256), F32), jax.ShapeDtypeStruct((4, 128), F32)),
-        in_specs=[held] * 2,
+        in_specs=[vmem] * 2,
         out_specs=(held, held),
         scratch_shapes=[pltpu.SemaphoreType.DMA((2,))],
-        compiler_params=pltpu.CompilerParams(vmem_limit_bytes=60 << 20),
+        compiler_params=pltpu.CompilerParams(vmem_limit_bytes=40 << 20),
         name="hand_on",
     )(moments, residual)
     return moments, residual.reshape(512)

time: 108 us -> 107 us (level)
  no operation moved by 1% of the time
where the time goes in v6:
time: 107 us
  Pallas kernels  106 us (99%)
  between operations  1.29 us (1%)
    pallas_call x1, Pallas kernels, local(): pl.pallas_call(functools.partial(kernel, sizes), out_shape=(jax.ShapeDtyp...  105 us

profile of v6, /device:TPU:1, one launch (start us, length us, event | category | flops | bytes accessed | tf_op | source)
XLA Modules:
  0.0 106.9 jit_solution(4636059976971010191)
XLA Ops:
  1.3 105.0 %solve.1 = (f32[3,256]{1,0:T(4,128)S(1)}, f32[4,128]{1,0:T(4,128)S(1)}) custom-call(f32[4,128]{1,0:T(4,128)} %bitcast.2, s32[3,256]{1,0:T(4,128)} %grains_in.1, s32[3,32768]{1,0:T(4,128)} %pixels_in.1, s32[1,36]{1,0:T(1,128)} %block_grain_in.1, s32[1,36]{1,0:T(1,128)} %block_pixel_in.1, s32[1,1]{1,0:T(1,128)S(6)} %copy.8.block_count_in), custom_call_target="tpu_custom_call" | custom-call | tf_op jit(solution)/shard_map/solve/pallas_call | solution.py:413
  106.3 0.6 hand_on.1

commit v7 on v6

--- a/solution.py
+++ b/solution.py
@@ -11,7 +11,7 @@
 BLOCK_G = 64
 ITERS = 3
 SLOTS = 36
-UNROLL = 6
+UNROLL = 12
 GROUPS = 8
 F32 = jnp.float32
 

time: 107 us -> 107 us (level)
  no operation moved by 1% of the time
where the time goes in v7:
time: 107 us
  Pallas kernels  105 us (98%)
  between operations  1.29 us (1%)
    pallas_call x1, Pallas kernels, local(): pl.pallas_call(functools.partial(kernel, sizes), out_shape=(jax.ShapeDtyp...  105 us

profile of v7, /device:TPU:1, one launch (start us, length us, event | category | flops | bytes accessed | tf_op | source)
XLA Modules:
  0.0 106.7 jit_solution(13453469096789914760)
XLA Ops:
  1.3 104.8 %solve.1 = (f32[3,256]{1,0:T(4,128)S(1)}, f32[4,128]{1,0:T(4,128)S(1)}) custom-call(f32[4,128]{1,0:T(4,128)} %bitcast.2, s32[3,256]{1,0:T(4,128)} %grains_in.1, s32[3,32768]{1,0:T(4,128)} %pixels_in.1, s32[1,36]{1,0:T(1,128)} %block_grain_in.1, s32[1,36]{1,0:T(1,128)} %block_pixel_in.1, s32[1,1]{1,0:T(1,128)S(6)} %copy.8.block_count_in), custom_call_target="tpu_custom_call" | custom-call | tf_op jit(solution)/shard_map/solve/pallas_call | solution.py:413
  106.1 0.6 hand_on.1
